TPU v7x, 32 devices: a whole 2x2x4 slice. The times are simulated.
32 devices in a mesh: gx: 2 (over x), gy: 4 (over z), gz: 4 (over y, core).
Axes of the slice: x: 2, y: 2, z: 4, core: 2. Of those that a mesh axis runs over, the one named last changes fastest.
Arguments:
- initial_block: float32 [64, 32, 32, 256], P(None, 'gz', 'gy', 'gx'), may hold values from -6 to 6
- phase_map: int32 [32, 32, 256], P('gz', 'gy', 'gx'), may hold values from 0 to 3
- phase_density: float32 [4], replicated, may hold values from 0.5 to 4
- phase_modulus: float32 [4], replicated, may hold values from 0.5 to 4
- bloch_sign: int32 [32, 256], P('gy', 'gx'), may hold values from -1 to 1, as said below
Outputs:
- ritz_basis: float32 [64, 32, 32, 256], P(None, 'gz', 'gy', 'gx')
- projected: float32 [64, 64], replicated
Inputs may be any that keep to these rules, and one draw needn't show every extreme that they name: `bloch_sign`: each entry is -1 or +1.
All inputs are finite; a program needn't handle non-finite values.
Results may differ from a plain program's by a relative error of at most 0.00011.
Values sent between devices are 32-bit elements; how exact they have to be, the bound alone decides.
A program may use at most 128 MiB of HBM per device.

v0:
```python
import jax
import jax.numpy as jnp
from jax import lax
from jax.sharding import PartitionSpec as P

DEGREE = 6


def extended(block, sides, width):
    for axis, dim in sides:
        count = lax.axis_size(axis)
        forward = [(i, i + 1) for i in range(count - 1)]
        forward.append((count - 1, 0))
        backward = [(target, source) for source, target in forward]
        low = lax.ppermute(
            lax.slice_in_dim(block, block.shape[dim] - width, None, axis=dim), axis, forward
        )
        high = lax.ppermute(lax.slice_in_dim(block, 0, width, axis=dim), axis, backward)
        block = jnp.concatenate([low, block, high], axis=dim)
    return block


def lookup(phase_map, table):
    hits = phase_map[..., None] == jnp.arange(table.shape[0], dtype=jnp.int32)
    return jnp.sum(jnp.where(hits, table, jnp.float32(0.0)), axis=-1)


def gram(left, right):
    rows = left.shape[0]
    return jnp.dot(
        left.reshape(rows, -1), right.reshape(rows, -1).T, precision=lax.Precision.HIGHEST
    )


def stiffness(block, rho_pad, low_factor, high_factor):
    padded = extended(block, (("gx", 3), ("gy", 2), ("gz", 1)), 1)
    padded = padded.at[:, 0, 1:-1, 1:-1].multiply(low_factor[None])
    padded = padded.at[:, -1, 1:-1, 1:-1].multiply(high_factor[None])
    centre = padded[:, 1:-1, 1:-1, 1:-1]
    inv_rho = rho_pad[1:-1, 1:-1, 1:-1]
    w_up = 0.5 * (inv_rho + rho_pad[2:, 1:-1, 1:-1])
    w_down = 0.5 * (inv_rho + rho_pad[:-2, 1:-1, 1:-1])
    total = w_up * (centre - padded[:, 2:, 1:-1, 1:-1]) + w_down * (
        centre - padded[:, :-2, 1:-1, 1:-1]
    )
    w_up = 0.5 * (inv_rho + rho_pad[1:-1, 2:, 1:-1])
    w_down = 0.5 * (inv_rho + rho_pad[1:-1, :-2, 1:-1])
    total = total + (
        w_up * (centre - padded[:, 1:-1, 2:, 1:-1]) + w_down * (centre - padded[:, 1:-1, :-2, 1:-1])
    )
    w_up = 0.5 * (inv_rho + rho_pad[1:-1, 1:-1, 2:])
    w_down = 0.5 * (inv_rho + rho_pad[1:-1, 1:-1, :-2])
    total = total + (
        w_up * (centre - padded[:, 1:-1, 1:-1, 2:]) + w_down * (centre - padded[:, 1:-1, 1:-1, :-2])
    )
    return total


def body(initial_block, phase_map, phase_density, phase_modulus, bloch_sign):
    inv_rho = lookup(phase_map, 1.0 / phase_density)
    kappa = lookup(phase_map, phase_modulus)
    sign = bloch_sign.astype(jnp.float32)
    z_index = lax.axis_index("gz")
    z_count = lax.axis_size("gz")
    low_factor = jnp.where(z_index == 0, sign, jnp.float32(1.0))
    high_factor = jnp.where(z_index == z_count - 1, sign, jnp.float32(1.0))
    rho_pad = extended(inv_rho, (("gx", 2), ("gy", 1), ("gz", 0)), 1)
    top = 12.0 * jnp.max(phase_modulus) * jnp.max(1.0 / phase_density)
    low = 0.03 * top
    centre = (top + low) / 2.0
    half = (top - low) / 2.0
    cells = (
        initial_block.shape[1]
        * initial_block.shape[2]
        * initial_block.shape[3]
        * lax.axis_size("gx")
        * lax.axis_size("gy")
        * z_count
    )
    current = initial_block
    lap = kappa * stiffness(current, rho_pad, low_factor, high_factor)
    following = (lap - centre * current) / half
    previous, current = (current, following)
    for step in range(DEGREE - 1):
        lap = kappa * stiffness(current, rho_pad, low_factor, high_factor)
        following = 2.0 * (lap - centre * current) / half - previous
        previous, current = (current, following)
    correlation_local = gram(current / kappa[None], current)
    applied = stiffness(current, rho_pad, low_factor, high_factor)
    energy_local = gram(current, applied)
    correlation_total, energy_total = lax.psum(
        (correlation_local, energy_local), ("gx", "gy", "gz")
    )
    correlation = correlation_total / cells
    energy = energy_total / cells
    rows = current.shape[0]
    factor = jnp.linalg.cholesky(correlation)
    inverse = jax.scipy.linalg.solve_triangular(
        factor, jnp.eye(rows, dtype=jnp.float32), lower=True
    )
    basis = jnp.dot(inverse, current.reshape(rows, -1), precision=lax.Precision.HIGHEST).reshape(
        current.shape
    )
    projected = jnp.dot(
        jnp.dot(inverse, energy, precision=lax.Precision.HIGHEST),
        inverse.T,
        precision=lax.Precision.HIGHEST,
    )
    return (basis, projected)


def solution(mesh):
    in_specs = (P(None, "gz", "gy", "gx"), P("gz", "gy", "gx"), P(), P(), P("gy", "gx"))
    out_specs = (P(None, "gz", "gy", "gx"), P())
    return jax.shard_map(body, mesh=mesh, in_specs=in_specs, out_specs=out_specs, check_vma=False)
```

profile of v0, /device:TPU:0, one launch (start us, length us, event | category | flops | bytes accessed | tf_op | source)
XLA Modules:
  0.0 1980.2 jit_solution(10078879603563903501)
XLA Ops:
  88.8 86.9 %scatter-mul.46 = f32[64,10,10,130]{3,1,2,0:T(8,128)} dynamic-update-slice(f32[64,10,10,130]{3,1,2,0:T(8,128)} %pad_maximum_fusion, f32[64,1,8,128]{3,1,2,0:T(1,128)} %copy.195, s32[]{:T(128)} %constant.380.clone.1, s32[]{:T(128)} %constant.380.clone.1, s32[]{:T(128)} %constant.381.clone.1, s32[]{:T(128)} %constant.381.clone.1) | dynamic-update-slice | bytes 524292 | tf_op jit(solution)/shard_map/scatter-mul | solution.py:37
  178.5 87.5 %scatter-mul.49 = f32[64,10,10,130]{3,1,2,0:T(8,128)} dynamic-update-slice(f32[64,10,10,130]{3,1,2,0:T(8,128)} %scatter-mul.46, f32[64,1,8,128]{3,1,2,0:T(1,128)S(1)} %slice_multiply_fusion.12, s32[]{:T(128)} %constant.380.clone.1, s32[]{:T(128)} %constant.383.clone.1, s32[]{:T(128)} %constant.381.clone.1, s32[]{:T(128)} %constant.381.clone.1) | dynamic-update-slice | bytes 524292 | tf_op jit(solution)/shard_map/scatter-mul | solution.py:38
  266.0 19.6 fusion.96
  357.8 87.4 %scatter-mul.50 = f32[64,10,10,130]{3,1,2,0:T(8,128)} dynamic-update-slice(f32[64,10,10,130]{3,1,2,0:T(8,128)} %pad_maximum_fusion.1, f32[64,1,8,128]{3,1,2,0:T(1,128)S(1)} %copy.211, s32[]{:T(128)} %constant.380.clone.1, s32[]{:T(128)} %constant.380.clone.1, s32[]{:T(128)} %constant.381.clone.1, s32[]{:T(128)} %constant.381.clone.1) | dynamic-update-slice | bytes 524292 | tf_op jit(solution)/shard_map/scatter-mul | solution.py:37
  448.1 87.5 %scatter-mul.51 = f32[64,10,10,130]{3,1,2,0:T(8,128)} dynamic-update-slice(f32[64,10,10,130]{3,1,2,0:T(8,128)} %scatter-mul.50, f32[64,1,8,128]{3,1,2,0:T(1,128)S(1)} %slice_multiply_fusion.10, s32[]{:T(128)} %constant.380.clone.1, s32[]{:T(128)} %constant.383.clone.1, s32[]{:T(128)} %constant.381.clone.1, s32[]{:T(128)} %constant.381.clone.1) | dynamic-update-slice | bytes 524292 | tf_op jit(solution)/shard_map/scatter-mul | solution.py:38
  535.6 20.8 %fusion.82 = f32[64,8,8,128]{3,1,2,0:T(8,128)} fusion(f32[64,10,10,130]{3,1,2,0:T(8,128)} %scatter-mul.51, f32[64,8,8,128]{3,1,2,0:T(8,128)S(1)} %fusion.96, f32[]{:T(128)S(6)} %div.58, f32[]{:T(128)S(6)} %div.57, f32[8,8,128]{2,0,1:T(8,128)S(1)} %copy.200, f32[8,8,128]{2,0,1:T(8,128)S(1)} %copy.199, f32[8,8,128]{2,0,1:T(8,128)S(1)} %copy.198, ...), kind=kLoop, calls=%fused_computation.121 | loop fusion | flops 12058624 | bytes 21200904 | tf_op jit(solution)/shard_map/sub | solution.py:86
  630.2 87.4 %scatter-mul.54 = f32[64,10,10,130]{3,1,2,0:T(8,128)} dynamic-update-slice(f32[64,10,10,130]{3,1,2,0:T(8,128)} %pad_maximum_fusion.2, f32[64,1,8,128]{3,1,2,0:T(1,128)S(1)} %copy.222, s32[]{:T(128)} %constant.380.clone.1, s32[]{:T(128)} %constant.380.clone.1, s32[]{:T(128)} %constant.381.clone.1, s32[]{:T(128)} %constant.381.clone.1) | dynamic-update-slice | bytes 524292 | tf_op jit(solution)/shard_map/scatter-mul | solution.py:37
  720.4 87.5 %scatter-mul.55 = f32[64,10,10,130]{3,1,2,0:T(8,128)} dynamic-update-slice(f32[64,10,10,130]{3,1,2,0:T(8,128)} %scatter-mul.54, f32[64,1,8,128]{3,1,2,0:T(1,128)S(1)} %slice_multiply_fusion.8, s32[]{:T(128)} %constant.380.clone.1, s32[]{:T(128)} %constant.383.clone.1, s32[]{:T(128)} %constant.381.clone.1, s32[]{:T(128)} %constant.381.clone.1) | dynamic-update-slice | bytes 524292 | tf_op jit(solution)/shard_map/scatter-mul | solution.py:38
  807.9 21.0 %fusion.66 = f32[64,8,8,128]{3,1,2,0:T(8,128)} fusion(f32[64,8,8,128]{3,1,2,0:T(8,128)S(1)} %fusion.96, f32[64,10,10,130]{3,1,2,0:T(8,128)} %scatter-mul.55, f32[64,8,8,128]{3,1,2,0:T(8,128)} %fusion.82, f32[]{:T(128)S(6)} %div.58, f32[]{:T(128)S(6)} %div.57, f32[8,8,128]{2,0,1:T(8,128)S(1)} %copy.200, f32[8,8,128]{2,0,1:T(8,128)S(1)} %copy.199, ...), kind=kLoop, calls=%fused_computation.99 | loop fusion | flops 12058624 | bytes 21200904 | tf_op jit(solution)/shard_map/sub | solution.py:86
  879.6 13.5 collective-permute-done.28
  902.1 87.4 %scatter-mul.56 = f32[64,10,10,130]{3,1,2,0:T(8,128)} dynamic-update-slice(f32[64,10,10,130]{3,1,2,0:T(8,128)} %pad_maximum_fusion.3, f32[64,1,8,128]{3,1,2,0:T(1,128)S(1)} %copy.232, s32[]{:T(128)} %constant.380.clone.1, s32[]{:T(128)} %constant.380.clone.1, s32[]{:T(128)} %constant.381.clone.1, s32[]{:T(128)} %constant.381.clone.1) | dynamic-update-slice | bytes 524292 | tf_op jit(solution)/shard_map/scatter-mul | solution.py:37
  992.4 87.5 %scatter-mul.59 = f32[64,10,10,130]{3,1,2,0:T(8,128)} dynamic-update-slice(f32[64,10,10,130]{3,1,2,0:T(8,128)} %scatter-mul.56, f32[64,1,8,128]{3,1,2,0:T(1,128)S(1)} %slice_multiply_fusion.6, s32[]{:T(128)} %constant.380.clone.1, s32[]{:T(128)} %constant.383.clone.1, s32[]{:T(128)} %constant.381.clone.1, s32[]{:T(128)} %constant.381.clone.1) | dynamic-update-slice | bytes 524292 | tf_op jit(solution)/shard_map/scatter-mul | solution.py:38
  1079.9 20.8 %fusion.50 = f32[64,8,8,128]{3,1,2,0:T(8,128)S(1)} fusion(f32[64,8,8,128]{3,1,2,0:T(8,128)} %fusion.82, f32[64,10,10,130]{3,1,2,0:T(8,128)} %scatter-mul.59, f32[64,8,8,128]{3,1,2,0:T(8,128)} %fusion.66, f32[]{:T(128)S(6)} %div.58, f32[]{:T(128)S(6)} %div.57, f32[8,8,128]{2,0,1:T(8,128)S(1)} %copy.200, f32[8,8,128]{2,0,1:T(8,128)S(1)} %copy.199, ...), kind=kLoop, calls=%fused_computation.77 | loop fusion | flops 12058624 | bytes 21200904 | tf_op jit(solution)/shard_map/sub | solution.py:86
  1150.7 13.5 collective-permute-done.34
  1173.0 87.4 %scatter-mul.60 = f32[64,10,10,130]{3,1,2,0:T(8,128)} dynamic-update-slice(f32[64,10,10,130]{3,1,2,0:T(8,128)} %pad_maximum_fusion.4, f32[64,1,8,128]{3,1,2,0:T(1,128)S(1)} %copy.242, s32[]{:T(128)} %constant.380.clone.1, s32[]{:T(128)} %constant.380.clone.1, s32[]{:T(128)} %constant.381.clone.1, s32[]{:T(128)} %constant.381.clone.1) | dynamic-update-slice | bytes 524292 | tf_op jit(solution)/shard_map/scatter-mul | solution.py:37
  1263.3 87.5 %scatter-mul.61 = f32[64,10,10,130]{3,1,2,0:T(8,128)} dynamic-update-slice(f32[64,10,10,130]{3,1,2,0:T(8,128)} %scatter-mul.60, f32[64,1,8,128]{3,1,2,0:T(1,128)S(1)} %slice_multiply_fusion.4, s32[]{:T(128)} %constant.380.clone.1, s32[]{:T(128)} %constant.383.clone.1, s32[]{:T(128)} %constant.381.clone.1, s32[]{:T(128)} %constant.381.clone.1) | dynamic-update-slice | bytes 524292 | tf_op jit(solution)/shard_map/scatter-mul | solution.py:38
  1350.8 20.6 %fusion.34 = f32[64,8,8,128]{3,1,2,0:T(8,128)} fusion(f32[64,8,8,128]{3,1,2,0:T(8,128)} %fusion.66, f32[64,10,10,130]{3,1,2,0:T(8,128)} %scatter-mul.61, f32[64,8,8,128]{3,1,2,0:T(8,128)S(1)} %fusion.50, f32[]{:T(128)S(6)} %div.58, f32[]{:T(128)S(6)} %div.57, f32[8,8,128]{2,0,1:T(8,128)S(1)} %copy.200, f32[8,8,128]{2,0,1:T(8,128)S(1)} %copy.199, ...), kind=kLoop, calls=%fused_computation.55 | loop fusion | flops 12058624 | bytes 21200904 | tf_op jit(solution)/shard_map/sub | solution.py:86
  1443.5 87.4 %scatter-mul.64 = f32[64,10,10,130]{3,1,2,0:T(8,128)} dynamic-update-slice(f32[64,10,10,130]{3,1,2,0:T(8,128)} %pad_maximum_fusion.5, f32[64,1,8,128]{3,1,2,0:T(1,128)S(1)} %copy.252, s32[]{:T(128)} %constant.380.clone.1, s32[]{:T(128)} %constant.380.clone.1, s32[]{:T(128)} %constant.381.clone.1, s32[]{:T(128)} %constant.381.clone.1) | dynamic-update-slice | bytes 524292 | tf_op jit(solution)/shard_map/scatter-mul | solution.py:37
  1533.7 87.5 %scatter-mul.65 = f32[64,10,10,130]{3,1,2,0:T(8,128)} dynamic-update-slice(f32[64,10,10,130]{3,1,2,0:T(8,128)} %scatter-mul.64, f32[64,1,8,128]{3,1,2,0:T(1,128)S(1)} %slice_multiply_fusion.2, s32[]{:T(128)} %constant.380.clone.1, s32[]{:T(128)} %constant.383.clone.1, s32[]{:T(128)} %constant.381.clone.1, s32[]{:T(128)} %constant.381.clone.1) | dynamic-update-slice | bytes 524292 | tf_op jit(solution)/shard_map/scatter-mul | solution.py:38
  1621.2 21.8 %broadcast_divide_fusion = (f32[64,8,8,128]{3,1,2,0:T(8,128)}, f32[64,8,8,128]{3,1,2,0:T(8,128)S(1)}) fusion(f32[8,8,128]{2,0,1:T(8,128)S(1)} %copy.183, f32[64,8,8,128]{3,1,2,0:T(8,128)} %copy-done, f32[]{:T(128)S(6)} %div.58, f32[64,8,8,128]{3,1,2,0:T(8,128)} %fusion.34, f32[]{:T(128)S(6)} %div.57, f32[64,10,10,130]{3,1,2,0:T(8,128)} %scatter-mul.65, ...), kind=kLoop, calls=%fused_computation.165 | loop fusion | flops 12582912 | bytes 23298056 | tf_op jit(solution)/shard_map/div | solution.py:88
  1714.9 87.4 %scatter-mul.66 = f32[64,10,10,130]{3,1,2,0:T(8,128)} dynamic-update-slice(f32[64,10,10,130]{3,1,2,0:T(8,128)} %pad_maximum_fusion.6, f32[64,1,8,128]{3,1,2,0:T(1,128)S(1)} %copy.268, s32[]{:T(128)} %constant.380.clone.1, s32[]{:T(128)} %constant.380.clone.1, s32[]{:T(128)} %constant.381.clone.1, s32[]{:T(128)} %constant.381.clone.1) | dynamic-update-slice | bytes 524292 | tf_op jit(solution)/shard_map/scatter-mul | solution.py:37
  1805.2 87.5 %scatter-mul.69 = f32[64,10,10,130]{3,1,2,0:T(8,128)} dynamic-update-slice(f32[64,10,10,130]{3,1,2,0:T(8,128)} %scatter-mul.66, f32[64,1,8,128]{3,1,2,0:T(1,128)S(1)} %slice_multiply_fusion, s32[]{:T(128)} %constant.380.clone.1, s32[]{:T(128)} %constant.383.clone.1, s32[]{:T(128)} %constant.381.clone.1, s32[]{:T(128)} %constant.381.clone.1) | dynamic-update-slice | bytes 524292 | tf_op jit(solution)/shard_map/scatter-mul | solution.py:38
  1892.6 19.9 %fusion.2 = f32[64,8,8,128]{3,1,2,0:T(8,128)} fusion(f32[64,10,10,130]{3,1,2,0:T(8,128)} %scatter-mul.69, f32[8,8,128]{2,0,1:T(8,128)S(1)} %copy.200, f32[8,8,128]{2,0,1:T(8,128)S(1)} %copy.199, f32[8,8,128]{2,0,1:T(8,128)S(1)} %copy.198, f32[8,8,128]{2,0,1:T(8,128)S(1)} %copy.197, f32[8,8,128]{2,0,1:T(8,128)S(1)} %copy.196, f32[8,8,128]{2,0,1:T(8,128)S(1)} %copy.184), kind=kLoop, calls=%fused_computation.11 | loop fusion | flops 8912896 | bytes 16973824 | tf_op jit(solution)/shard_map/add | solution.py:53
  1918.2 41.0 %all-reduce = (f32[64,64]{0,1:T(8,128)S(1)}, f32[64,64]{0,1:T(8,128)S(1)}) all-reduce(f32[64,64]{0,1:T(8,128)S(1)} %fusion.113, f32[64,64]{0,1:T(8,128)S(1)} %fusion.118), channel_id=1, replica_groups=mesh['gx'=2,'gy'=4,'gz'=4] {'gx','gy','gz'}, use_global_device_ids=true, to_apply=%region_4.5 | all-reduce | flops 8192 | bytes 65536 | tf_op jit(solution)/shard_map/psum | solution.py:91
  (280 shorter events, 540.5 us)
Async XLA Ops:
  2.8 17.3 collective-permute-start.1
  20.3 18.4 collective-permute-start.3
  32.9 16.9 collective-permute-start.7
  32.9 23.7 %collective-permute-start.8 = (f32[64,8,1,130]{3,1,2,0:T(8,128)}, f32[64,8,1,130]{3,1,2,0:T(8,128)S(1)}, u32[]{:S(2)}, u32[]{:S(2)}) collective-permute-start(f32[64,8,1,130]{3,1,2,0:T(8,128)} %get-tuple-element.215), channel_id=1, source_target_pairs={{4,0},{8,4},{12,8},{0,12},{5,1},{9,5},{13,9},{1,13},{6,2},{10,6},{... | collective-permute-start | bytes 798728 | tf_op jit(solution)/shard_map/ppermute | solution.py:18
  38.8 27.7 %collective-permute-start.4 = (f32[1,10,130]{2,1,0:T(8,128)S(1)}, f32[1,10,130]{2,1,0:T(8,128)S(1)}, u32[]{:S(2)}, u32[]{:S(2)}) collective-permute-start(f32[1,10,130]{2,1,0:T(8,128)S(1)} %get-tuple-element.232), channel_id=1, source_target_pairs={{1,0},{2,1},{3,2},{0,3},{5,4},{6,5},{7,6},{4,7},{9,8},{10,9},{11,1... | collective-permute-start | bytes 15608 | tf_op jit(solution)/shard_map/ppermute | solution.py:18
  38.8 27.7 %collective-permute-start.11 = (f32[1,10,130]{2,1,0:T(8,128)S(1)}, f32[1,10,130]{2,1,0:T(8,128)S(1)}, u32[]{:S(2)}, u32[]{:S(2)}) collective-permute-start(f32[1,10,130]{2,1,0:T(8,128)S(1)} %get-tuple-element.233), channel_id=1, source_target_pairs={{0,1},{1,2},{2,3},{3,0},{4,5},{5,6},{6,7},{7,4},{8,9},{9,10},{10,1... | collective-permute-start | bytes 15608 | tf_op jit(solution)/shard_map/ppermute | solution.py:15
  64.7 16.4 collective-permute-start.10
  303.7 16.8 collective-permute-start.14
  306.1 23.7 %collective-permute-start.15 = (f32[64,8,1,130]{3,1,2,0:T(8,128)S(1)}, f32[64,8,1,130]{3,1,2,0:T(8,128)S(1)}, u32[]{:S(2)}, u32[]{:S(2)}) collective-permute-start(f32[64,8,1,130]{3,1,2,0:T(8,128)S(1)} %get-tuple-element.213), channel_id=1, source_target_pairs={{4,0},{8,4},{12,8},{0,12},{5,1},{9,5},{13,9},{1,13},{6,2},{10,6},{... | collective-permute-start | bytes 798728 | tf_op jit(solution)/shard_map/ppermute | solution.py:18
  334.2 16.1 collective-permute-start.17
  576.9 16.7 collective-permute-start.20
  577.5 24.4 %collective-permute-start.21 = (f32[64,8,1,130]{3,1,2,0:T(8,128)S(1)}, f32[64,8,1,130]{3,1,2,0:T(8,128)S(1)}, u32[]{:S(2)}, u32[]{:S(2)}) collective-permute-start(f32[64,8,1,130]{3,1,2,0:T(8,128)S(1)} %get-tuple-element.211), channel_id=1, source_target_pairs={{4,0},{8,4},{12,8},{0,12},{5,1},{9,5},{13,9},{1,13},{6,2},{10,6},{... | collective-permute-start | bytes 798728 | tf_op jit(solution)/shard_map/ppermute | solution.py:18
  847.5 16.7 collective-permute-start.26
  848.8 24.6 %collective-permute-start.27 = (f32[64,8,1,130]{3,1,2,0:T(8,128)S(1)}, f32[64,8,1,130]{3,1,2,0:T(8,128)S(1)}, u32[]{:S(2)}, u32[]{:S(2)}) collective-permute-start(f32[64,8,1,130]{3,1,2,0:T(8,128)S(1)} %get-tuple-element.209), channel_id=1, source_target_pairs={{4,0},{8,4},{12,8},{0,12},{5,1},{9,5},{13,9},{1,13},{6,2},{10,6},{... | collective-permute-start | bytes 798728 | tf_op jit(solution)/shard_map/ppermute | solution.py:18
  877.8 16.4 collective-permute-start.29
  1118.9 16.7 collective-permute-start.32
  1120.4 24.1 %collective-permute-start.33 = (f32[64,8,1,130]{3,1,2,0:T(8,128)S(1)}, f32[64,8,1,130]{3,1,2,0:T(8,128)S(1)}, u32[]{:S(2)}, u32[]{:S(2)}) collective-permute-start(f32[64,8,1,130]{3,1,2,0:T(8,128)S(1)} %get-tuple-element.207), channel_id=1, source_target_pairs={{4,0},{8,4},{12,8},{0,12},{5,1},{9,5},{13,9},{1,13},{6,2},{10,6},{... | collective-permute-start | bytes 798728 | tf_op jit(solution)/shard_map/ppermute | solution.py:18
  1148.9 16.4 collective-permute-start.35
  1390.0 16.7 collective-permute-start.38
  1390.7 24.0 %collective-permute-start.39 = (f32[64,8,1,130]{3,1,2,0:T(8,128)S(1)}, f32[64,8,1,130]{3,1,2,0:T(8,128)S(1)}, u32[]{:S(2)}, u32[]{:S(2)}) collective-permute-start(f32[64,8,1,130]{3,1,2,0:T(8,128)S(1)} %get-tuple-element.205), channel_id=1, source_target_pairs={{4,0},{8,4},{12,8},{0,12},{5,1},{9,5},{13,9},{1,13},{6,2},{10,6},{... | collective-permute-start | bytes 798728 | tf_op jit(solution)/shard_map/ppermute | solution.py:18
  1419.1 16.4 collective-permute-start.41
  1661.2 16.7 collective-permute-start.44
  1662.4 24.1 %collective-permute-start.45 = (f32[64,8,1,130]{3,1,2,0:T(8,128)S(1)}, f32[64,8,1,130]{3,1,2,0:T(8,128)S(1)}, u32[]{:S(2)}, u32[]{:S(2)}) collective-permute-start(f32[64,8,1,130]{3,1,2,0:T(8,128)S(1)} %get-tuple-element.203), channel_id=1, source_target_pairs={{4,0},{8,4},{12,8},{0,12},{5,1},{9,5},{13,9},{1,13},{6,2},{10,6},{... | collective-permute-start | bytes 798728 | tf_op jit(solution)/shard_map/ppermute | solution.py:18
  1690.9 16.2 collective-permute-start.47
  (47 other events, 903.4 us)
where the time goes:
time: 1990 us; the launch traced here: 1980 us
  local copies, waits for them, and re-layouts  1350 us (68%)
  other arithmetic  277 us (14%)
  waiting for transfers between devices  234 us (12%)
  starting transfers between devices  62.9 us (3%)
  blocking collectives  41 us (2%)
    another operation x7, local copies, waits for them, and re-layouts, stiffness(): padded = padded.at[:, -1, 1:-1, 1:-1].multiply(high_factor[None])  612 us
    another operation x7, local copies, waits for them, and re-layouts, stiffness(): padded = padded.at[:, 0, 1:-1, 1:-1].multiply(low_factor[None])  612 us
    ppermute x24, waiting for transfers between devices, extended(): lax.ppermute(lax.slice_in_dim(block, block.shape[dim] - width, None, axis...  173 us
    sub x4, other arithmetic, body(): following = 2.0 * (lap - centre * current) / half - previous  83.2 us
    ppermute x24, waiting for transfers between devices, extended(): lax.ppermute(lax.slice_in_dim(block, 0, width, axis=dim), axis, backward)  61 us
    concatenate x8, other arithmetic, extended(): block = jnp.concatenate([low, block, high], axis=dim)  49.4 us
    slice x14, other arithmetic, extended(): lax.slice_in_dim(block, block.shape[dim] - width, None, axis=dim)  46.8 us
    ppermute x24, starting transfers between devices, extended(): lax.ppermute(lax.slice_in_dim(block, 0, width, axis=dim), axis, backward)  45 us
  transfers between devices with their start and end apart: 48, of which 27 were waited for; matrix products, arithmetic and copies ran while one was open for 4% of the time, Pallas kernels for 0%

commit v1 on v0

v1 whole, which is shorter than its diff:
```python
import functools

import jax
import jax.numpy as jnp
from jax import lax
from jax.experimental import pallas as pl
from jax.experimental.pallas import tpu as pltpu
from jax.sharding import PartitionSpec as P

DEGREE = 6
GROUPS = 2
SUB, LANE = 8, 128
MESH = pl.DeviceIdType.MESH


def lookup(phase_map, table):
    hits = phase_map[..., None] == jnp.arange(table.shape[0], dtype=jnp.int32)
    return jnp.sum(jnp.where(hits, table, jnp.float32(0.0)), axis=-1)


def filter_kernel(
    scal_ref, init_ref, rho_ref, kappa_ref, low_ref, high_ref,
    filt_ref, app_ref,
    wcoef, vcoef, sendz, sendy, sendx, haloz, haloy, halox, send_sem, recv_sem,
):
    rows, nz = init_ref.shape[0], init_ref.shape[1]
    size = rows // GROUPS
    spans = [(g * size, size) for g in range(GROUPS)] + [(rows, 1)]
    gx, gy, gz = (lax.axis_index(a) for a in ("gx", "gy", "gz"))
    cx, cy, cz = (lax.axis_size(a) for a in ("gx", "gy", "gz"))
    other_x = (lax.rem(gx + 1, cx), gy, gz)
    y_up = (gx, lax.rem(gy + 1, cy), gz)
    y_down = (gx, lax.rem(gy + cy - 1, cy), gz)
    z_up = (gx, gy, lax.rem(gz + 1, cz))
    z_down = (gx, gy, lax.rem(gz + cz - 1, cz))

    barrier = pltpu.get_barrier_semaphore()
    for device in (other_x, y_up, y_down, z_up, z_down):
        pl.semaphore_signal(barrier, inc=1, device_id=device, device_id_type=MESH)
    pl.semaphore_wait(barrier, 5)

    lane = lax.broadcasted_iota(jnp.int32, (SUB, LANE), 1)
    sub = lax.broadcasted_iota(jnp.int32, (SUB, LANE), 0)

    def copies(slot, g):
        start, length = spans[g]
        part = pl.ds(start, length)
        plan = (
            (sendy.at[0, part], haloy.at[slot, 1, part], y_down),
            (sendy.at[1, part], haloy.at[slot, 0, part], y_up),
            (sendz.at[0, part], haloz.at[slot, 1, part], z_down),
            (sendz.at[1, part], haloz.at[slot, 0, part], z_up),
            (sendx.at[part], halox.at[slot, part], other_x),
        )
        return [
            pltpu.make_async_remote_copy(
                src_ref=src, dst_ref=dst,
                send_sem=send_sem.at[g, i], recv_sem=recv_sem.at[slot, g, i],
                device_id=device, device_id_type=MESH,
            )
            for i, (src, dst, device) in enumerate(plan)
        ]

    def pack(tiles, k):
        sendz[0, k] = tiles[0]
        sendz[1, k] = tiles[-1]
        packed = jnp.zeros((SUB, LANE), jnp.float32)
        for z, tile in enumerate(tiles):
            sendy[0, k, z : z + 1, :] = tile[0:1]
            sendy[1, k, z : z + 1, :] = tile[SUB - 1 : SUB]
            first = pltpu.roll(tile, 2 * z, 1) if z else tile
            packed = jnp.where(lane == 2 * z, first, packed)
            packed = jnp.where(lane == 2 * z + 1, pltpu.roll(tile, 2 * z + 2, 1), packed)
        sendx[k] = packed

    def neighbours(tiles, k, slot, z):
        tile = tiles[z]
        up = tiles[z + 1] if z + 1 < nz else haloz[slot, 1, k]
        down = tiles[z - 1] if z else haloz[slot, 0, k]
        y_after = jnp.where(
            sub == SUB - 1, haloy[slot, 1, k, z : z + 1, :], pltpu.roll(tile, SUB - 1, 0)
        )
        y_before = jnp.where(sub == 0, haloy[slot, 0, k, z : z + 1, :], pltpu.roll(tile, 1, 0))
        edge = pltpu.roll(halox[slot, k], LANE - 2 * z - 1, 1)
        x_after = jnp.where(lane == LANE - 1, edge, pltpu.roll(tile, LANE - 1, 1))
        x_before = jnp.where(lane == 0, edge, pltpu.roll(tile, 1, 1))
        return up, down, y_after, y_before, x_after, x_before

    def send(slot, g):
        for copy in copies(slot, g):
            copy.start()

    def arrive(slot, g):
        for copy in copies(slot, g):
            copy.wait()

    pack([rho_ref[z] for z in range(nz)], rows)
    send(0, GROUPS)
    for g in range(GROUPS):
        start, length = spans[g]

        def first(i, carry):
            k = start + i
            pack([init_ref[k, z] for z in range(nz)], k)
            return carry

        lax.fori_loop(0, length, first, 0)
        send(0, g)

    arrive(0, GROUPS)
    scale, shift = scal_ref[0], scal_ref[1]
    tiles = [rho_ref[z] for z in range(nz)]
    for z in range(nz):
        weights = [0.5 * (tiles[z] + n) for n in neighbours(tiles, rows, 0, z)]
        total = weights[0] + weights[1]
        for w in weights[2:]:
            total = total + w
        if z == nz - 1:
            weights[0] = weights[0] * high_ref[...]
        if z == 0:
            weights[1] = weights[1] * low_ref[...]
        factor = scale * kappa_ref[z]
        for i, w in enumerate(weights):
            wcoef[i, z] = w
            vcoef[i, z] = factor * w
        wcoef[6, z] = total
        vcoef[6, z] = factor * total - shift

    for step in range(DEGREE + 1):
        slot = step % 2
        last = step == DEGREE
        current = init_ref if step == 0 else (app_ref if step % 2 else filt_ref)
        target = app_ref if step % 2 == 0 else filt_ref
        previous = None
        if 0 < step < DEGREE:
            previous = init_ref if step == 1 else target
        coef = wcoef if last else vcoef
        for g in range(GROUPS):
            start, length = spans[g]
            arrive(slot, g)

            def one(i, carry):
                k = start + i
                tiles = [current[k, z] for z in range(nz)]
                made = []
                for z in range(nz):
                    around = neighbours(tiles, k, slot, z)
                    terms = [coef[j, z] * n for j, n in enumerate(around)]
                    pairs = (terms[0] + terms[1]) + (terms[2] + terms[3])
                    value = coef[6, z] * tiles[z] - (pairs + (terms[4] + terms[5]))
                    if step == 0:
                        value = 0.5 * value
                    if previous is not None:
                        value = value - previous[k, z]
                    made.append(value)
                for z in range(nz):
                    target[k, z] = made[z]
                if not last:
                    pack(made, k)
                return carry

            lax.fori_loop(0, length, one, 0)
            if not last:
                send(1 - slot, g)


def filtered_block(scal, block, inv_rho, kappa, low, high):
    rows = block.shape[0]
    vmem = pl.BlockSpec(memory_space=pltpu.VMEM)
    nz = block.shape[1]
    f32 = jnp.float32
    return pl.pallas_call(
        filter_kernel,
        out_shape=[jax.ShapeDtypeStruct(block.shape, f32)] * 2,
        in_specs=[pl.BlockSpec(memory_space=pltpu.SMEM)] + [vmem] * 5,
        out_specs=[vmem] * 2,
        scratch_shapes=[
            pltpu.VMEM((7, nz, SUB, LANE), f32),
            pltpu.VMEM((7, nz, SUB, LANE), f32),
            pltpu.VMEM((2, rows + 1, SUB, LANE), f32),
            pltpu.VMEM((2, rows + 1, SUB, LANE), f32),
            pltpu.VMEM((rows + 1, SUB, LANE), f32),
            pltpu.VMEM((2, 2, rows + 1, SUB, LANE), f32),
            pltpu.VMEM((2, 2, rows + 1, SUB, LANE), f32),
            pltpu.VMEM((2, rows + 1, SUB, LANE), f32),
            pltpu.SemaphoreType.DMA((GROUPS + 1, 5)),
            pltpu.SemaphoreType.DMA((2, GROUPS + 1, 5)),
        ],
        compiler_params=pltpu.CompilerParams(
            collective_id=0, has_side_effects=True, vmem_limit_bytes=40 * 1024 * 1024
        ),
    )(scal, block, inv_rho, kappa, low, high)


def gram(left, right):
    rows = left.shape[0]
    return jnp.dot(
        left.reshape(rows, -1), right.reshape(rows, -1).T, precision=lax.Precision.HIGHEST
    )


def body(initial_block, phase_map, phase_density, phase_modulus, bloch_sign):
    inv_rho = lookup(phase_map, 1.0 / phase_density)
    kappa = lookup(phase_map, phase_modulus)
    sign = bloch_sign.astype(jnp.float32)
    z_index = lax.axis_index("gz")
    z_count = lax.axis_size("gz")
    low_factor = jnp.where(z_index == 0, sign, jnp.float32(1.0))
    high_factor = jnp.where(z_index == z_count - 1, sign, jnp.float32(1.0))
    top = 12.0 * jnp.max(phase_modulus) * jnp.max(1.0 / phase_density)
    low = 0.03 * top
    centre = (top + low) / 2.0
    half = (top - low) / 2.0
    cells = (
        initial_block.shape[1]
        * initial_block.shape[2]
        * initial_block.shape[3]
        * lax.axis_size("gx")
        * lax.axis_size("gy")
        * z_count
    )
    scal = jnp.stack([2.0 / half, 2.0 * centre / half])
    current, applied = filtered_block(scal, initial_block, inv_rho, kappa, low_factor, high_factor)
    correlation_local = gram(current / kappa[None], current)
    energy_local = gram(current, applied)
    correlation_total, energy_total = lax.psum(
        (correlation_local, energy_local), ("gx", "gy", "gz")
    )
    correlation = correlation_total / cells
    energy = energy_total / cells
    rows = current.shape[0]
    factor = jnp.linalg.cholesky(correlation)
    inverse = jax.scipy.linalg.solve_triangular(
        factor, jnp.eye(rows, dtype=jnp.float32), lower=True
    )
    basis = jnp.dot(inverse, current.reshape(rows, -1), precision=lax.Precision.HIGHEST).reshape(
        current.shape
    )
    projected = jnp.dot(
        jnp.dot(inverse, energy, precision=lax.Precision.HIGHEST),
        inverse.T,
        precision=lax.Precision.HIGHEST,
    )
    return (basis, projected)


def solution(mesh):
    in_specs = (P(None, "gz", "gy", "gx"), P("gz", "gy", "gx"), P(), P(), P("gy", "gx"))
    out_specs = (P(None, "gz", "gy", "gx"), P())
    return jax.shard_map(body, mesh=mesh, in_specs=in_specs, out_specs=out_specs, check_vma=False)
```

time: 1990 us -> 177 us (0.09)
  local copies, waits for them, and re-layouts: 1350 us -> 5.77 us
  other arithmetic: 277 us -> 16.5 us
  waiting for transfers between devices: 234 us -> 0 us
  Pallas kernels: 0 us -> 98.8 us
  starting transfers between devices: 62.9 us -> 0 us
    another operation x14 -> x0, local copies, waits for them, and re-layouts: 1220 us -> none  [the longest x7 612 us: stiffness(): padded = padded.at[:, -1, 1:-1, 1:-1].multiply(high_factor[None])]
    ppermute x48 -> x0, waiting for transfers between devices: 234 us -> none  [the longest x24 173 us: extended(): lax.ppermute(lax.slice_in_dim(block, block.shape[dim] - width, None, axis...]
    pallas_call x0 -> x1, Pallas kernels: none -> 98.8 us  [filtered_block(): pl.pallas_call(filter_kernel, out_shape=[jax.ShapeDtypeStruct(block.shape...]
    sub x4 -> x0, other arithmetic: 83.2 us -> none  [body(): following = 2.0 * (lap - centre * current) / half - previous]
    ppermute x48 -> x0, starting transfers between devices: 62.9 us -> none  [the longest x24 45 us: extended(): lax.ppermute(lax.slice_in_dim(block, 0, width, axis=dim), axis, backward)]
    slice x34 -> x0, local copies, waits for them, and re-layouts: 56.6 us -> none  [the longest x20 43.1 us: extended(): lax.slice_in_dim(block, block.shape[dim] - width, None, axis=dim)]
    ppermute x28 -> x0, local copies, waits for them, and re-layouts: 50 us -> none  [the longest x14 25.1 us: extended(): lax.ppermute(lax.slice_in_dim(block, block.shape[dim] - width, None, axis...]
    concatenate x8 -> x0, other arithmetic: 49.4 us -> none  [extended(): block = jnp.concatenate([low, block, high], axis=dim)]
  transfers between devices with their start and end apart: 48 -> 0, of which waited for: 27 -> 0; matrix products, arithmetic and copies ran while one was open for 4% -> 0% of each run, Pallas kernels for 0% -> 0%
where the time goes in v1:
time: 177 us; the launch traced here: 176 us
  Pallas kernels  98.8 us (56%)
  blocking collectives  40.8 us (23%)
  other arithmetic  16.5 us (9%)
  matrix products  12.3 us (7%)
  local copies, waits for them, and re-layouts  5.77 us (3%)
  between operations  2.14 us (1%)
    pallas_call x1, Pallas kernels, filtered_block(): pl.pallas_call(filter_kernel, out_shape=[jax.ShapeDtypeStruct(block.shape...  98.8 us
    psum x1, blocking collectives, body(): lax.psum((correlation_local, energy_local), ('gx', 'gy', 'gz'))  40.8 us
    dot_general x2, matrix products, gram(): jnp.dot(left.reshape(rows, -1), right.reshape(rows, -1).T, precision=lax....  8.06 us
    another operation x3, other arithmetic, body(): factor = jnp.linalg.cholesky(correlation)  6.52 us
    unnamed x5, local copies, waits for them, and re-layouts  5.69 us
    another operation x2, other arithmetic, body(): jax.scipy.linalg.solve_triangular(factor, jnp.eye(rows, dtype=jnp.float32...  5.55 us

profile of v1, /device:TPU:0, one launch (start us, length us, event | category | flops | bytes accessed | tf_op | source)
XLA Modules:
  0.0 176.3 jit_solution(2009853286497557865)
XLA Ops:
  0.6 1.3 reduce_max.18
  2.6 1.3 fusion.27
  4.6 0.1 pad_maximum_fusion.scal_ref
  4.6 0.7 convert_select_fusion
  5.3 0.9 select_reduce_fusion
  6.2 0.0 copy-start
  6.2 1.6 copy-done
  7.8 98.8 %shard_map.68 = (f32[64,8,8,128]{3,2,1,0:T(8,128)S(1)}, f32[64,8,8,128]{3,2,1,0:T(8,128)S(1)}) custom-call(f32[2]{0:T(128)S(1)} %pad_maximum_fusion.scal_ref, f32[64,8,8,128]{3,2,1,0:T(8,128)S(1)} %copy-done, f32[8,8,128]{2,1,0:T(8,128)S(1)} %get-tuple-element.13.rho_ref, f32[8,8,128]{2,1,0:T(8,128)S(1)} %get-tuple-element.12.kappa_ref, ...), custom_call_target="tpu_custom_call" | custom-call | tf_op jit(solution)/shard_map/pallas_call | solution.py:172
  106.6 4.0 %fusion.13 = f32[64,64]{0,1:T(8,128)S(1)} fusion(f32[64,8,8,128]{3,2,1,0:T(8,128)S(1)} %get-tuple-element.5, f32[64,8,8,128]{3,2,1,0:T(8,128)S(1)} %get-tuple-element.4), kind=kOutput, calls=%fused_computation.10 | convolution fusion | flops 402653184 | bytes 4210688 | tf_op jit(solution)/shard_map/dot_general | solution.py:197
  110.6 0.2 broadcast_divide_fusion
  110.8 4.0 %fusion.8 = f32[64,64]{0,1:T(8,128)S(1)} fusion(f32[64,8,8,128]{3,2,1,0:T(8,128)S(1)} %get-tuple-element.4, f32[64,8,8,128]{3,2,1,0:T(8,128)S(1)} %broadcast_divide_fusion), kind=kOutput, calls=%fused_computation.9 | convolution fusion | flops 402653184 | bytes 4210688 | tf_op jit(solution)/shard_map/dot_general | solution.py:197
  114.9 40.8 %all-reduce = (f32[64,64]{0,1:T(8,128)S(1)}, f32[64,64]{0,1:T(8,128)S(1)}) all-reduce(f32[64,64]{0,1:T(8,128)S(1)} %fusion.8, f32[64,64]{0,1:T(8,128)S(1)} %fusion.13), channel_id=1, replica_groups=mesh['gx'=2,'gy'=4,'gz'=4] {'gx','gy','gz'}, use_global_device_ids=true, to_apply=%region_4.5 | all-reduce | flops 8192 | bytes 65536 | tf_op jit(solution)/shard_map/psum | solution.py:226
  155.7 0.1 copy.21
  155.8 5.8 %cholesky.17 = f32[64,64]{1,0:T(8,128)S(1)} custom-call(f32[64,64]{1,0:T(8,128)S(1)} %fusion.22), custom_call_target="Cholesky" | custom-call | tf_op jit(solution)/shard_map/jit(cholesky)/cholesky | solution.py:232
  161.7 0.6 compare_reduce_fusion
  162.3 0.7 fusion.18
  163.0 4.9 %custom-call.7 = f32[1,64,64]{1,2,0:T(8,128)S(1)} custom-call(f32[1,64,64]{2,1,0:T(8,128)S(1)} %fusion.18), custom_call_target="InvertDiagBlocksLowerTriangular" | custom-call | tf_op jit(solution)/shard_map/jit(_solve_triangular)/triangular_solve | solution.py:233
  167.9 0.2 fusion.20
  168.1 0.2 fusion.23
  168.3 0.8 fusion.28
  169.1 1.2 copy.53
  170.3 0.4 copy.33
  170.7 3.0 %fusion.2 = f32[64,8,8,128]{3,0,2,1:T(8,128)S(1)} fusion(f32[8,8,128,64]{2,1,0,3:T(8,128)S(1)} %bitcast.37, f32[64,64]{1,0:T(8,128)S(1)} %fusion.20), kind=kOutput, calls=%fused_computation.3 | convolution fusion | flops 402653184 | bytes 4210688 | tf_op jit(solution)/shard_map/dot_general | solution.py:236
  173.7 2.5 %copy.26 = f32[64,8,8,128]{3,2,1,0:T(8,128)} copy(f32[64,8,8,128]{3,0,2,1:T(8,128)S(1)} %fusion.2) | data formatting | bytes 4194304
  (3 shorter events, 0.0 us)
Async XLA Ops:
  6.2 1.6 copy-start

commit v2 on v1

--- a/solution.py
+++ b/solution.py
@@ -8,7 +8,7 @@
 from jax.sharding import PartitionSpec as P
 
 DEGREE = 6
-GROUPS = 2
+GROUPS = 4
 SUB, LANE = 8, 128
 MESH = pl.DeviceIdType.MESH
 
@@ -20,8 +20,8 @@
 
 def filter_kernel(
     scal_ref, init_ref, rho_ref, kappa_ref, low_ref, high_ref,
-    filt_ref, app_ref,
-    wcoef, vcoef, sendz, sendy, sendx, haloz, haloy, halox, send_sem, recv_sem,
+    filt_ref, both_ref,
+    app_ref, wcoef, vcoef, sendz, sendy, sendx, haloz, haloy, halox, send_sem, recv_sem,
 ):
     rows, nz = init_ref.shape[0], init_ref.shape[1]
     size = rows // GROUPS
@@ -124,6 +124,7 @@
             wcoef[i, z] = w
             vcoef[i, z] = factor * w
         wcoef[6, z] = total
+        wcoef[7, z] = 1.0 / kappa_ref[z]
         vcoef[6, z] = factor * total - shift
 
     for step in range(DEGREE + 1):
@@ -153,9 +154,13 @@
                     if previous is not None:
                         value = value - previous[k, z]
                     made.append(value)
-                for z in range(nz):
-                    target[k, z] = made[z]
-                if not last:
+                if last:
+                    for z in range(nz):
+                        both_ref[k, z] = tiles[z] * wcoef[7, z]
+                        both_ref[rows + k, z] = made[z]
+                else:
+                    for z in range(nz):
+                        target[k, z] = made[z]
                     pack(made, k)
                 return carry
 
@@ -171,11 +176,15 @@
     f32 = jnp.float32
     return pl.pallas_call(
         filter_kernel,
-        out_shape=[jax.ShapeDtypeStruct(block.shape, f32)] * 2,
+        out_shape=[
+            jax.ShapeDtypeStruct(block.shape, f32),
+            jax.ShapeDtypeStruct((2 * rows,) + block.shape[1:], f32),
+        ],
         in_specs=[pl.BlockSpec(memory_space=pltpu.SMEM)] + [vmem] * 5,
         out_specs=[vmem] * 2,
         scratch_shapes=[
-            pltpu.VMEM((7, nz, SUB, LANE), f32),
+            pltpu.VMEM(block.shape, f32),
+            pltpu.VMEM((8, nz, SUB, LANE), f32),
             pltpu.VMEM((7, nz, SUB, LANE), f32),
             pltpu.VMEM((2, rows + 1, SUB, LANE), f32),
             pltpu.VMEM((2, rows + 1, SUB, LANE), f32),
@@ -192,11 +201,112 @@
     )(scal, block, inv_rho, kappa, low, high)
 
 
-def gram(left, right):
-    rows = left.shape[0]
-    return jnp.dot(
-        left.reshape(rows, -1), right.reshape(rows, -1).T, precision=lax.Precision.HIGHEST
+def sum_kernel(local_ref, out_ref, *scratch):
+    axes = ("gx", "gy", "gz")
+    buffers, sends, arrivals = scratch[:3], scratch[3:6], scratch[6:9]
+    places = {a: lax.axis_index(a) for a in axes}
+    counts = {a: lax.axis_size(a) for a in axes}
+
+    def partner(axis, distance):
+        count = counts[axis]
+        place = dict(places)
+        place[axis] = lax.rem(places[axis] + distance, count)
+        return tuple(place[a] for a in axes)
+
+    barrier = pltpu.get_barrier_semaphore()
+    greeted = 0
+    for axis in axes:
+        for distance in range(1, counts[axis]):
+            pl.semaphore_signal(
+                barrier, inc=1, device_id=partner(axis, distance), device_id_type=MESH
+            )
+            greeted += 1
+    pl.semaphore_wait(barrier, greeted)
+
+    value = local_ref[...]
+    for axis, buffer, send_sem, recv_sem in zip(axes, buffers, sends, arrivals):
+        me = places[axis]
+        buffer[me] = value
+        started = []
+        for distance in range(1, counts[axis]):
+            copy = pltpu.make_async_remote_copy(
+                src_ref=buffer.at[me], dst_ref=buffer.at[me],
+                send_sem=send_sem.at[distance], recv_sem=recv_sem.at[distance],
+                device_id=partner(axis, distance), device_id_type=MESH,
+            )
+            copy.start()
+            started.append(copy)
+        for distance, copy in enumerate(started, 1):
+            copy.wait_send()
+            source = lax.rem(me + counts[axis] - distance, counts[axis])
+            pltpu.make_async_remote_copy(
+                src_ref=buffer.at[source], dst_ref=buffer.at[source],
+                send_sem=send_sem.at[distance], recv_sem=recv_sem.at[distance],
+                device_id=partner(axis, distance), device_id_type=MESH,
+            ).wait_recv()
+        value = buffer[0]
+        for i in range(1, counts[axis]):
+            value = value + buffer[i]
+    out_ref[...] = value
+
+
+def sum_over_devices(local):
+    counts = [lax.axis_size(a) for a in ("gx", "gy", "gz")]
+    vmem = pl.BlockSpec(memory_space=pltpu.VMEM)
+    return pl.pallas_call(
+        sum_kernel,
+        out_shape=jax.ShapeDtypeStruct(local.shape, jnp.float32),
+        in_specs=[vmem],
+        out_specs=vmem,
+        scratch_shapes=[pltpu.VMEM((n,) + local.shape, jnp.float32) for n in counts]
+        + [pltpu.SemaphoreType.DMA((n,)) for n in counts] * 2,
+        compiler_params=pltpu.CompilerParams(collective_id=1, has_side_effects=True),
+    )(local)
+
+
+def project_kernel(cells, sums_ref, inverse_ref, projected_ref):
+    rows = sums_ref.shape[0]
+    sums = sums_ref[...] * (1.0 / cells)
+    correlation, energy = sums[:, :rows], sums[:, rows:]
+    correlation = 0.5 * (correlation + correlation.T)
+    row_index = lax.broadcasted_iota(jnp.int32, (rows, rows), 0)
+    column_index = lax.broadcasted_iota(jnp.int32, (rows, rows), 1)
+    eye = jnp.where(row_index == column_index, jnp.float32(1.0), jnp.float32(0.0))
+    work = jnp.concatenate([correlation, eye], axis=1)
+    blocks = [work[i : i + SUB] for i in range(0, rows, SUB)]
+    sub = lax.broadcasted_iota(jnp.int32, (SUB, 2 * rows), 0)
+    for j in range(rows):
+        own, at = divmod(j, SUB)
+        columns = {
+            b: jnp.broadcast_to(blocks[b][:, j : j + 1], (SUB, 2 * rows))
+            for b in range(own, len(blocks))
+        }
+        ratio = blocks[own][at : at + 1] / columns[own][at : at + 1]
+        for b in range(own, len(blocks)):
+            updated = blocks[b] - columns[b] * ratio
+            blocks[b] = jnp.where(sub > at, updated, blocks[b]) if b == own else updated
+    work = jnp.concatenate(blocks, axis=0)
+    pivots = jnp.sum(
+        jnp.where(row_index == column_index, work[:, :rows], jnp.float32(0.0)),
+        axis=1, keepdims=True,
     )
+    inverse = work[:, rows:] / jnp.sqrt(pivots)
+    inverse_ref[...] = inverse
+    half_way = jnp.dot(inverse, energy, precision=lax.Precision.HIGHEST)
+    projected_ref[...] = lax.dot_general(
+        half_way, inverse, (((1,), (1,)), ((), ())), precision=lax.Precision.HIGHEST
+    )
+
+
+def project(sums, cells):
+    rows = sums.shape[0]
+    vmem = pl.BlockSpec(memory_space=pltpu.VMEM)
+    return pl.pallas_call(
+        functools.partial(project_kernel, cells),
+        out_shape=[jax.ShapeDtypeStruct((rows, rows), jnp.float32)] * 2,
+        in_specs=[vmem],
+        out_specs=[vmem] * 2,
+    )(sums)
 
 
 def body(initial_block, phase_map, phase_density, phase_modulus, bloch_sign):
@@ -220,27 +330,12 @@
         * z_count
     )
     scal = jnp.stack([2.0 / half, 2.0 * centre / half])
-    current, applied = filtered_block(scal, initial_block, inv_rho, kappa, low_factor, high_factor)
-    correlation_local = gram(current / kappa[None], current)
-    energy_local = gram(current, applied)
-    correlation_total, energy_total = lax.psum(
-        (correlation_local, energy_local), ("gx", "gy", "gz")
-    )
-    correlation = correlation_total / cells
-    energy = energy_total / cells
+    current, both = filtered_block(scal, initial_block, inv_rho, kappa, low_factor, high_factor)
     rows = current.shape[0]
-    factor = jnp.linalg.cholesky(correlation)
-    inverse = jax.scipy.linalg.solve_triangular(
-        factor, jnp.eye(rows, dtype=jnp.float32), lower=True
-    )
-    basis = jnp.dot(inverse, current.reshape(rows, -1), precision=lax.Precision.HIGHEST).reshape(
-        current.shape
-    )
-    projected = jnp.dot(
-        jnp.dot(inverse, energy, precision=lax.Precision.HIGHEST),
-        inverse.T,
-        precision=lax.Precision.HIGHEST,
-    )
+    flat = current.reshape(rows, -1)
+    local = jnp.dot(flat, both.reshape(2 * rows, -1).T, precision=lax.Precision.HIGHEST)
+    inverse, projected = project(sum_over_devices(local), cells)
+    basis = jnp.dot(inverse, flat, precision=lax.Precision.HIGHEST).reshape(current.shape)
     return (basis, projected)
 
 

time: 177 us -> 136 us (0.77)
  blocking collectives: 40.8 us -> 0 us
  Pallas kernels: 98.8 us -> 112 us
  other arithmetic: 16.5 us -> 4.16 us
    psum x1 -> x0, blocking collectives: 40.8 us -> none  [body(): lax.psum((correlation_local, energy_local), ('gx', 'gy', 'gz'))]
    pallas_call x0 -> x2, Pallas kernels: none -> 21 us  [the longest x1 13.7 us: sum_over_devices(): pl.pallas_call(sum_kernel, out_shape=jax.ShapeDtypeStruct(local.shape, jn...]
    another operation x5 -> x0, other arithmetic: 12.1 us -> none  [the longest x3 6.52 us: body(): factor = jnp.linalg.cholesky(correlation)]
    pallas_call x1, Pallas kernels: 98.8 us -> 90.7 us  [filtered_block(): pl.pallas_call(filter_kernel, out_shape=[jax.ShapeDtypeStruct(block.shape...]
    dot_general x5 -> x2, matrix products: 12.1 us -> 11.6 us  [the longest x1 7.79 us: body(): jnp.dot(flat, both.reshape(2 * rows, -1).T, precision=lax.Precision.HIGHEST)]
where the time goes in v2:
time: 136 us; the launch traced here: 135 us
  Pallas kernels  112 us (82%)
  matrix products  11.6 us (9%)
  local copies, waits for them, and re-layouts  5.69 us (4%)
  other arithmetic  4.16 us (3%)
  between operations  2.08 us (2%)
    pallas_call x1, Pallas kernels, filtered_block(): pl.pallas_call(filter_kernel, out_shape=[jax.ShapeDtypeStruct(block.shape...  90.7 us
    pallas_call x1, Pallas kernels, sum_over_devices(): pl.pallas_call(sum_kernel, out_shape=jax.ShapeDtypeStruct(local.shape, jn...  13.7 us
    dot_general x1, matrix products, body(): jnp.dot(flat, both.reshape(2 * rows, -1).T, precision=lax.Precision.HIGHEST)  7.79 us
    pallas_call x1, Pallas kernels, project(): pl.pallas_call(functools.partial(project_kernel, cells), out_shape=[jax.S...  7.26 us
    unnamed x5, local copies, waits for them, and re-layouts  5.69 us
    dot_general x1, matrix products, body(): jnp.dot(inverse, flat, precision=lax.Precision.HIGHEST)  3.8 us

profile of v2, /device:TPU:0, one launch (start us, length us, event | category | flops | bytes accessed | tf_op | source)
XLA Modules:
  0.0 135.2 jit_solution(7987926867675450795)
XLA Ops:
  0.6 1.3 reduce_max.18
  2.6 1.3 fusion.11
  4.6 0.1 pad_maximum_fusion.scal_ref
  4.6 0.7 convert_select_fusion
  5.3 0.9 select_reduce_fusion
  6.2 0.0 copy-start
  6.2 1.6 %copy-done = f32[64,8,8,128]{3,2,1,0:T(8,128)S(1)} copy-done((f32[64,8,8,128]{3,2,1,0:T(8,128)S(1)}, f32[64,8,8,128]{3,2,1,0:T(8,128)}, u32[]{:S(2)}) %copy-start) | copy-done | bytes 2097176
  7.8 90.7 %shard_map.68 = (f32[64,8,8,128]{3,2,1,0:T(8,128)S(1)}, f32[128,8,8,128]{3,2,1,0:T(8,128)S(1)}) custom-call(f32[2]{0:T(128)S(1)} %pad_maximum_fusion.scal_ref, f32[64,8,8,128]{3,2,1,0:T(8,128)S(1)} %copy-done, f32[8,8,128]{2,1,0:T(8,128)S(1)} %get-tuple-element.17.rho_ref, f32[8,8,128]{2,1,0:T(8,128)S(1)} %get-tuple-element.16.kappa_ref, ...), custom_call_target="tpu_custom_call" | custom-call | tf_op jit(solution)/shard_map/pallas_call | solution.py:177
  98.5 7.8 %fusion.5.local_ref = f32[64,128]{1,0:T(8,128)} fusion(f32[128,8,8,128]{3,2,1,0:T(8,128)S(1)} %get-tuple-element.7, f32[64,8,8,128]{3,2,1,0:T(8,128)S(1)} %get-tuple-element.6), kind=kOutput, calls=%fused_computation.6 | convolution fusion | flops 805306368 | bytes 6324224 | tf_op jit(solution)/shard_map/dot_general | solution.py:336
  106.3 13.7 %shard_map.69.sums_ref = f32[64,128]{1,0:T(8,128)} custom-call(f32[64,128]{1,0:T(8,128)} %fusion.5.local_ref), custom_call_target="tpu_custom_call" | custom-call | tf_op jit(solution)/shard_map/pallas_call | solution.py:256
  120.0 1.2 copy.33
  121.2 0.4 copy.21
  121.6 7.3 %shard_map.70 = (f32[64,64]{1,0:T(8,128)}, f32[64,64]{1,0:T(8,128)}) custom-call(f32[64,128]{1,0:T(8,128)} %shard_map.69.sums_ref), custom_call_target="tpu_custom_call" | custom-call | tf_op jit(solution)/shard_map/pallas_call | solution.py:304
  128.9 3.8 %fusion.2 = f32[64,8,8,128]{3,0,2,1:T(8,128)S(1)} fusion(f32[8,8,128,64]{2,1,0,3:T(8,128)S(1)} %bitcast.25, f32[64,64]{1,0:T(8,128)} %get-tuple-element.8), kind=kOutput, calls=%fused_computation.3 | convolution fusion | flops 402653184 | bytes 4210688 | tf_op jit(solution)/shard_map/dot_general | solution.py:338
  132.7 2.5 %copy.17 = f32[64,8,8,128]{3,2,1,0:T(8,128)} copy(f32[64,8,8,128]{3,0,2,1:T(8,128)S(1)} %fusion.2) | data formatting | bytes 4194304
Async XLA Ops:
  6.2 1.6 %copy-start = (f32[64,8,8,128]{3,2,1,0:T(8,128)S(1)}, f32[64,8,8,128]{3,2,1,0:T(8,128)}, u32[]{:S(2)}) copy-start(f32[64,8,8,128]{3,2,1,0:T(8,128)} %init_ref.1) | copy-start | bytes 6291460

commit v3 on v2

--- a/solution.py
+++ b/solution.py
@@ -9,17 +9,13 @@
 
 DEGREE = 6
 GROUPS = 4
+UNROLL = 2
 SUB, LANE = 8, 128
 MESH = pl.DeviceIdType.MESH
 
 
-def lookup(phase_map, table):
-    hits = phase_map[..., None] == jnp.arange(table.shape[0], dtype=jnp.int32)
-    return jnp.sum(jnp.where(hits, table, jnp.float32(0.0)), axis=-1)
-
-
 def filter_kernel(
-    scal_ref, init_ref, rho_ref, kappa_ref, low_ref, high_ref,
+    density_ref, modulus_ref, init_ref, phase_ref, sign_ref,
     filt_ref, both_ref,
     app_ref, wcoef, vcoef, sendz, sendy, sendx, haloz, haloy, halox, send_sem, recv_sem,
 ):
@@ -42,7 +38,7 @@
     lane = lax.broadcasted_iota(jnp.int32, (SUB, LANE), 1)
     sub = lax.broadcasted_iota(jnp.int32, (SUB, LANE), 0)
 
-    def copies(slot, g):
+    def copies(slot, g, one_way=False):
         start, length = spans[g]
         part = pl.ds(start, length)
         plan = (
@@ -59,6 +55,7 @@
                 device_id=device, device_id_type=MESH,
             )
             for i, (src, dst, device) in enumerate(plan)
+            if not (one_way and i in (1, 3))
         ]
 
     def pack(tiles, k):
@@ -68,63 +65,90 @@
         for z, tile in enumerate(tiles):
             sendy[0, k, z : z + 1, :] = tile[0:1]
             sendy[1, k, z : z + 1, :] = tile[SUB - 1 : SUB]
-            first = pltpu.roll(tile, 2 * z, 1) if z else tile
-            packed = jnp.where(lane == 2 * z, first, packed)
-            packed = jnp.where(lane == 2 * z + 1, pltpu.roll(tile, 2 * z + 2, 1), packed)
+            packed = jnp.where(lane // 2 == z, pltpu.roll(tile, 2 * z + 1, 1), packed)
         sendx[k] = packed
 
-    def neighbours(tiles, k, slot, z):
+    def neighbours(tiles, k, slot, z, one_way=False):
         tile = tiles[z]
-        up = tiles[z + 1] if z + 1 < nz else haloz[slot, 1, k]
-        down = tiles[z - 1] if z else haloz[slot, 0, k]
+        z_after = tiles[z + 1] if z + 1 < nz else haloz[slot, 1, k]
         y_after = jnp.where(
             sub == SUB - 1, haloy[slot, 1, k, z : z + 1, :], pltpu.roll(tile, SUB - 1, 0)
         )
+        edge = pltpu.roll(halox[slot, k], LANE - 2 * z - 1, 1)
+        x_after = pltpu.roll(jnp.where(lane == 0, edge, tile), LANE - 1, 1)
+        if one_way:
+            return z_after, y_after, x_after
+        z_before = tiles[z - 1] if z else haloz[slot, 0, k]
         y_before = jnp.where(sub == 0, haloy[slot, 0, k, z : z + 1, :], pltpu.roll(tile, 1, 0))
-        edge = pltpu.roll(halox[slot, k], LANE - 2 * z - 1, 1)
-        x_after = jnp.where(lane == LANE - 1, edge, pltpu.roll(tile, LANE - 1, 1))
-        x_before = jnp.where(lane == 0, edge, pltpu.roll(tile, 1, 1))
-        return up, down, y_after, y_before, x_after, x_before
-
-    def send(slot, g):
-        for copy in copies(slot, g):
+        x_before = pltpu.roll(jnp.where(lane == LANE - 1, edge, tile), 1, 1)
+        return z_after, y_after, x_after, z_before, y_before, x_before
+
+    def send(slot, g, one_way=False):
+        for copy in copies(slot, g, one_way):
             copy.start()
 
-    def arrive(slot, g):
-        for copy in copies(slot, g):
+    def arrive(slot, g, one_way=False):
+        for copy in copies(slot, g, one_way):
             copy.wait()
 
-    pack([rho_ref[z] for z in range(nz)], rows)
+    def filled(value):
+        return jnp.full((SUB, LANE), value, jnp.float32)
+
+    count = density_ref.shape[0]
+    densities = [1.0 / filled(density_ref[i]) for i in range(count)]
+    moduli = [filled(modulus_ref[i]) for i in range(count)]
+    phases = [phase_ref[z] for z in range(nz)]
+
+    def looked_up(phase, table):
+        value = jnp.zeros((SUB, LANE), jnp.float32)
+        for i, entry in enumerate(table):
+            value = jnp.where(phase == i, entry, value)
+        return value
+
+    rho = [looked_up(phase, densities) for phase in phases]
+    pack(rho, rows)
     send(0, GROUPS)
     for g in range(GROUPS):
         start, length = spans[g]
 
         def first(i, carry):
-            k = start + i
-            pack([init_ref[k, z] for z in range(nz)], k)
+            for u in range(UNROLL):
+                k = start + i * UNROLL + u
+                pack([init_ref[k, z] for z in range(nz)], k)
             return carry
 
-        lax.fori_loop(0, length, first, 0)
+        lax.fori_loop(0, length // UNROLL, first, 0)
         send(0, g)
 
+    top = 12.0 * functools.reduce(jnp.maximum, moduli) * functools.reduce(jnp.maximum, densities)
+    low = 0.03 * top
+    centre = (top + low) / 2.0
+    half = (top - low) / 2.0
+    scale, shift = 2.0 / half, 2.0 * centre / half
+    sign = sign_ref[...].astype(jnp.float32)
+    at_low = jnp.broadcast_to(gz, (SUB, LANE)) == 0
+    at_high = jnp.broadcast_to(gz, (SUB, LANE)) == cz - 1
+    low_sign = jnp.where(at_low, sign, jnp.float32(1.0))
+    high_sign = jnp.where(at_high, sign, jnp.float32(1.0))
+
     arrive(0, GROUPS)
-    scale, shift = scal_ref[0], scal_ref[1]
-    tiles = [rho_ref[z] for z in range(nz)]
     for z in range(nz):
-        weights = [0.5 * (tiles[z] + n) for n in neighbours(tiles, rows, 0, z)]
-        total = weights[0] + weights[1]
-        for w in weights[2:]:
-            total = total + w
+        kappa = looked_up(phases[z], moduli)
+        weights = [0.5 * (rho[z] + n) for n in neighbours(rho, rows, 0, z)]
+        total = weights[0] + weights[3]
+        total = total + (weights[1] + weights[4])
+        total = total + (weights[2] + weights[5])
         if z == nz - 1:
-            weights[0] = weights[0] * high_ref[...]
+            weights[0] = weights[0] * high_sign
         if z == 0:
-            weights[1] = weights[1] * low_ref[...]
-        factor = scale * kappa_ref[z]
+            weights[3] = weights[3] * low_sign
+        factor = scale * kappa
         for i, w in enumerate(weights):
-            wcoef[i, z] = w
+            if i < 3:
+                wcoef[i, z] = w
             vcoef[i, z] = factor * w
-        wcoef[6, z] = total
-        wcoef[7, z] = 1.0 / kappa_ref[z]
+        wcoef[3, z] = 0.5 * total
+        wcoef[4, z] = 1.0 / kappa
         vcoef[6, z] = factor * total - shift
 
     for step in range(DEGREE + 1):
@@ -135,41 +159,47 @@
         previous = None
         if 0 < step < DEGREE:
             previous = init_ref if step == 1 else target
-        coef = wcoef if last else vcoef
         for g in range(GROUPS):
             start, length = spans[g]
-            arrive(slot, g)
+            arrive(slot, g, last)
 
             def one(i, carry):
-                k = start + i
-                tiles = [current[k, z] for z in range(nz)]
-                made = []
+                ks = [start + i * UNROLL + u for u in range(UNROLL)]
+                fields = [[current[k, z] for z in range(nz)] for k in ks]
+                made = [[] for _ in ks]
                 for z in range(nz):
-                    around = neighbours(tiles, k, slot, z)
-                    terms = [coef[j, z] * n for j, n in enumerate(around)]
-                    pairs = (terms[0] + terms[1]) + (terms[2] + terms[3])
-                    value = coef[6, z] * tiles[z] - (pairs + (terms[4] + terms[5]))
-                    if step == 0:
-                        value = 0.5 * value
-                    if previous is not None:
-                        value = value - previous[k, z]
-                    made.append(value)
-                if last:
+                    for u, k in enumerate(ks):
+                        tiles = fields[u]
+                        around = neighbours(tiles, k, slot, z, last)
+                        if last:
+                            terms = [wcoef[j, z] * n for j, n in enumerate(around)]
+                            value = wcoef[3, z] * tiles[z] - ((terms[0] + terms[1]) + terms[2])
+                        else:
+                            terms = [vcoef[j, z] * n for j, n in enumerate(around)]
+                            pairs = (terms[0] + terms[3]) + (terms[1] + terms[4])
+                            value = vcoef[6, z] * tiles[z] - (pairs + (terms[2] + terms[5]))
+                        if step == 0:
+                            value = 0.5 * value
+                        if previous is not None:
+                            value = value - previous[k, z]
+                        made[u].append(value)
+                for u, k in enumerate(ks):
                     for z in range(nz):
-                        both_ref[k, z] = tiles[z] * wcoef[7, z]
-                        both_ref[rows + k, z] = made[z]
-                else:
-                    for z in range(nz):
-                        target[k, z] = made[z]
-                    pack(made, k)
+                        if last:
+                            both_ref[k, z] = fields[u][z] * wcoef[4, z]
+                            both_ref[rows + k, z] = made[u][z]
+                        else:
+                            target[k, z] = made[u][z]
+                    if not last:
+                        pack(made[u], k)
                 return carry
 
-            lax.fori_loop(0, length, one, 0)
+            lax.fori_loop(0, length // UNROLL, one, 0)
             if not last:
-                send(1 - slot, g)
-
-
-def filtered_block(scal, block, inv_rho, kappa, low, high):
+                send(1 - slot, g, step == DEGREE - 1)
+
+
+def filtered_block(density, modulus, block, phase, sign):
     rows = block.shape[0]
     vmem = pl.BlockSpec(memory_space=pltpu.VMEM)
     nz = block.shape[1]
@@ -180,11 +210,11 @@
             jax.ShapeDtypeStruct(block.shape, f32),
             jax.ShapeDtypeStruct((2 * rows,) + block.shape[1:], f32),
         ],
-        in_specs=[pl.BlockSpec(memory_space=pltpu.SMEM)] + [vmem] * 5,
+        in_specs=[pl.BlockSpec(memory_space=pltpu.SMEM)] * 2 + [vmem] * 3,
         out_specs=[vmem] * 2,
         scratch_shapes=[
             pltpu.VMEM(block.shape, f32),
-            pltpu.VMEM((8, nz, SUB, LANE), f32),
+            pltpu.VMEM((5, nz, SUB, LANE), f32),
             pltpu.VMEM((7, nz, SUB, LANE), f32),
             pltpu.VMEM((2, rows + 1, SUB, LANE), f32),
             pltpu.VMEM((2, rows + 1, SUB, LANE), f32),
@@ -198,7 +228,7 @@
         compiler_params=pltpu.CompilerParams(
             collective_id=0, has_side_effects=True, vmem_limit_bytes=40 * 1024 * 1024
         ),
-    )(scal, block, inv_rho, kappa, low, high)
+    )(density, modulus, block, phase, sign)
 
 
 def sum_kernel(local_ref, out_ref, *scratch):
@@ -269,6 +299,7 @@
     sums = sums_ref[...] * (1.0 / cells)
     correlation, energy = sums[:, :rows], sums[:, rows:]
     correlation = 0.5 * (correlation + correlation.T)
+    energy = energy + energy.T
     row_index = lax.broadcasted_iota(jnp.int32, (rows, rows), 0)
     column_index = lax.broadcasted_iota(jnp.int32, (rows, rows), 1)
     eye = jnp.where(row_index == column_index, jnp.float32(1.0), jnp.float32(0.0))
@@ -310,17 +341,7 @@
 
 
 def body(initial_block, phase_map, phase_density, phase_modulus, bloch_sign):
-    inv_rho = lookup(phase_map, 1.0 / phase_density)
-    kappa = lookup(phase_map, phase_modulus)
-    sign = bloch_sign.astype(jnp.float32)
-    z_index = lax.axis_index("gz")
     z_count = lax.axis_size("gz")
-    low_factor = jnp.where(z_index == 0, sign, jnp.float32(1.0))
-    high_factor = jnp.where(z_index == z_count - 1, sign, jnp.float32(1.0))
-    top = 12.0 * jnp.max(phase_modulus) * jnp.max(1.0 / phase_density)
-    low = 0.03 * top
-    centre = (top + low) / 2.0
-    half = (top - low) / 2.0
     cells = (
         initial_block.shape[1]
         * initial_block.shape[2]
@@ -329,8 +350,9 @@
         * lax.axis_size("gy")
         * z_count
     )
-    scal = jnp.stack([2.0 / half, 2.0 * centre / half])
-    current, both = filtered_block(scal, initial_block, inv_rho, kappa, low_factor, high_factor)
+    current, both = filtered_block(
+        phase_density, phase_modulus, initial_block, phase_map, bloch_sign
+    )
     rows = current.shape[0]
     flat = current.reshape(rows, -1)
     local = jnp.dot(flat, both.reshape(2 * rows, -1).T, precision=lax.Precision.HIGHEST)

time: 136 us -> 127 us (0.934)
  Pallas kernels: 112 us -> 106 us
  other arithmetic: 4.16 us -> 0 us
  local copies, waits for them, and re-layouts: 5.69 us -> 8.44 us
  between operations: 2.08 us -> 0.68 us
    pallas_call x1, Pallas kernels: 90.7 us -> 85.3 us  [filtered_block(): pl.pallas_call(filter_kernel, out_shape=[jax.ShapeDtypeStruct(block.shape...]
    unnamed x5 -> x13, local copies, waits for them, and re-layouts: 5.69 us -> 8.44 us
    reduce_max x2 -> x0, other arithmetic: 2.53 us -> none  [body(): top = 12.0 * jnp.max(phase_modulus) * jnp.max(1.0 / phase_density)]
where the time goes in v3:
time: 127 us; the launch traced here: 126 us
  Pallas kernels  106 us (83%)
  matrix products  11.6 us (9%)
  local copies, waits for them, and re-layouts  8.44 us (7%)
    pallas_call x1, Pallas kernels, filtered_block(): pl.pallas_call(filter_kernel, out_shape=[jax.ShapeDtypeStruct(block.shape...  85.3 us
    pallas_call x1, Pallas kernels, sum_over_devices(): pl.pallas_call(sum_kernel, out_shape=jax.ShapeDtypeStruct(local.shape, jn...  13.1 us
    unnamed x13, local copies, waits for them, and re-layouts  8.44 us
    dot_general x1, matrix products, body(): jnp.dot(flat, both.reshape(2 * rows, -1).T, precision=lax.Precision.HIGHEST)  7.79 us
    pallas_call x1, Pallas kernels, project(): pl.pallas_call(functools.partial(project_kernel, cells), out_shape=[jax.S...  7.26 us
    dot_general x1, matrix products, body(): jnp.dot(inverse, flat, precision=lax.Precision.HIGHEST)  3.8 us

profile of v3, /device:TPU:0, one launch (start us, length us, event | category | flops | bytes accessed | tf_op | source)
XLA Modules:
  0.0 126.4 jit_solution(3838816262564833271)
XLA Ops:
  0.6 0.0 copy-start
  0.6 1.6 %copy-done = f32[64,8,8,128]{3,2,1,0:T(8,128)S(1)} copy-done((f32[64,8,8,128]{3,2,1,0:T(8,128)S(1)}, f32[64,8,8,128]{3,2,1,0:T(8,128)}, u32[]{:S(2)}) %copy-start) | copy-done | bytes 2097176
  2.2 0.0 copy-start.1
  2.2 0.8 copy-done.1
  3.0 0.0 copy-start.2
  3.0 0.7 copy-done.2
  3.7 0.0 copy-start.3
  3.7 0.7 copy-done.3
  4.3 0.0 copy-start.4
  4.3 0.7 copy-done.4
  5.0 85.3 %shard_map.68 = (f32[64,8,8,128]{3,2,1,0:T(8,128)S(1)}, f32[128,8,8,128]{3,2,1,0:T(8,128)S(1)}) custom-call(f32[4]{0:T(128)S(1)} %copy-done.3, f32[4]{0:T(128)S(1)} %copy-done.4, f32[64,8,8,128]{3,2,1,0:T(8,128)S(1)} %copy-done, s32[8,8,128]{2,1,0:T(8,128)S(1)} %copy-done.1, s32[8,128]{1,0:T(8,128)S(1)} %copy-done.2), custom_call_target="tpu_custom_call" | custom-call | tf_op jit(solution)/shard_map/pallas_call | solution.py:207
  90.3 7.8 %fusion.5.local_ref = f32[64,128]{1,0:T(8,128)} fusion(f32[128,8,8,128]{3,2,1,0:T(8,128)S(1)} %get-tuple-element.7, f32[64,8,8,128]{3,2,1,0:T(8,128)S(1)} %get-tuple-element.6), kind=kOutput, calls=%fused_computation.6 | convolution fusion | flops 805306368 | bytes 6324224 | tf_op jit(solution)/shard_map/dot_general | solution.py:358
  98.1 13.1 %shard_map.69.sums_ref = f32[64,128]{1,0:T(8,128)} custom-call(f32[64,128]{1,0:T(8,128)} %fusion.5.local_ref), custom_call_target="tpu_custom_call" | custom-call | tf_op jit(solution)/shard_map/pallas_call | solution.py:286
  111.2 1.2 copy.29
  112.4 0.4 copy.17
  112.8 7.3 %shard_map.70 = (f32[64,64]{1,0:T(8,128)}, f32[64,64]{1,0:T(8,128)}) custom-call(f32[64,128]{1,0:T(8,128)} %shard_map.69.sums_ref), custom_call_target="tpu_custom_call" | custom-call | tf_op jit(solution)/shard_map/pallas_call | solution.py:335
  120.0 3.8 %fusion.2 = f32[64,8,8,128]{3,0,2,1:T(8,128)S(1)} fusion(f32[8,8,128,64]{2,1,0,3:T(8,128)S(1)} %bitcast.23, f32[64,64]{1,0:T(8,128)} %get-tuple-element.8), kind=kOutput, calls=%fused_computation.3 | convolution fusion | flops 402653184 | bytes 4210688 | tf_op jit(solution)/shard_map/dot_general | solution.py:360
  123.8 2.5 %copy.13 = f32[64,8,8,128]{3,2,1,0:T(8,128)} copy(f32[64,8,8,128]{3,0,2,1:T(8,128)S(1)} %fusion.2) | data formatting | bytes 4194304
Async XLA Ops:
  0.6 1.6 %copy-start = (f32[64,8,8,128]{3,2,1,0:T(8,128)S(1)}, f32[64,8,8,128]{3,2,1,0:T(8,128)}, u32[]{:S(2)}) copy-start(f32[64,8,8,128]{3,2,1,0:T(8,128)} %init_ref.1) | copy-start | bytes 6291460
  2.2 0.8 copy-start.1
  3.0 0.7 copy-start.2
  3.7 0.7 copy-start.3
  4.3 0.7 copy-start.4

commit v4 on v3

--- a/solution.py
+++ b/solution.py
@@ -231,7 +231,7 @@
     )(density, modulus, block, phase, sign)
 
 
-def sum_kernel(local_ref, out_ref, *scratch):
+def sum_kernel(cells, local_ref, inverse_ref, projected_ref, *scratch):
     axes = ("gx", "gy", "gz")
     buffers, sends, arrivals = scratch[:3], scratch[3:6], scratch[6:9]
     places = {a: lax.axis_index(a) for a in axes}
@@ -277,26 +277,27 @@
         value = buffer[0]
         for i in range(1, counts[axis]):
             value = value + buffer[i]
-    out_ref[...] = value
-
-
-def sum_over_devices(local):
+    project_sums(cells, value, inverse_ref, projected_ref)
+
+
+def sum_and_project(local, cells):
+    rows = local.shape[0]
     counts = [lax.axis_size(a) for a in ("gx", "gy", "gz")]
     vmem = pl.BlockSpec(memory_space=pltpu.VMEM)
     return pl.pallas_call(
-        sum_kernel,
-        out_shape=jax.ShapeDtypeStruct(local.shape, jnp.float32),
+        functools.partial(sum_kernel, cells),
+        out_shape=[jax.ShapeDtypeStruct((rows, rows), jnp.float32)] * 2,
         in_specs=[vmem],
-        out_specs=vmem,
+        out_specs=[vmem] * 2,
         scratch_shapes=[pltpu.VMEM((n,) + local.shape, jnp.float32) for n in counts]
         + [pltpu.SemaphoreType.DMA((n,)) for n in counts] * 2,
         compiler_params=pltpu.CompilerParams(collective_id=1, has_side_effects=True),
     )(local)
 
 
-def project_kernel(cells, sums_ref, inverse_ref, projected_ref):
-    rows = sums_ref.shape[0]
-    sums = sums_ref[...] * (1.0 / cells)
+def project_sums(cells, sums, inverse_ref, projected_ref):
+    rows = sums.shape[0]
+    sums = sums * (1.0 / cells)
     correlation, energy = sums[:, :rows], sums[:, rows:]
     correlation = 0.5 * (correlation + correlation.T)
     energy = energy + energy.T
@@ -329,17 +330,6 @@
     )
 
 
-def project(sums, cells):
-    rows = sums.shape[0]
-    vmem = pl.BlockSpec(memory_space=pltpu.VMEM)
-    return pl.pallas_call(
-        functools.partial(project_kernel, cells),
-        out_shape=[jax.ShapeDtypeStruct((rows, rows), jnp.float32)] * 2,
-        in_specs=[vmem],
-        out_specs=[vmem] * 2,
-    )(sums)
-
-
 def body(initial_block, phase_map, phase_density, phase_modulus, bloch_sign):
     z_count = lax.axis_size("gz")
     cells = (
@@ -356,7 +346,7 @@
     rows = current.shape[0]
     flat = current.reshape(rows, -1)
     local = jnp.dot(flat, both.reshape(2 * rows, -1).T, precision=lax.Precision.HIGHEST)
-    inverse, projected = project(sum_over_devices(local), cells)
+    inverse, projected = sum_and_project(local, cells)
     basis = jnp.dot(inverse, flat, precision=lax.Precision.HIGHEST).reshape(current.shape)
     return (basis, projected)
 

time: 127 us -> 126 us (level)
  Pallas kernels: 106 us -> 104 us
    pallas_call x2 -> x1, Pallas kernels: 20.4 us -> 19 us  [sum_and_project(): pl.pallas_call(functools.partial(sum_kernel, cells), out_shape=[jax.Shape...]
    unnamed x13 -> x16, local copies, waits for them, and re-layouts: 8.44 us -> 9.06 us
where the time goes in v4:
time: 126 us
  Pallas kernels  104 us (83%)
  matrix products  11.6 us (9%)
  local copies, waits for them, and re-layouts  9.06 us (7%)
    pallas_call x1, Pallas kernels, filtered_block(): pl.pallas_call(filter_kernel, out_shape=[jax.ShapeDtypeStruct(block.shape...  85.3 us
    pallas_call x1, Pallas kernels, sum_and_project(): pl.pallas_call(functools.partial(sum_kernel, cells), out_shape=[jax.Shape...  19 us
    unnamed x16, local copies, waits for them, and re-layouts  9.06 us
    dot_general x1, matrix products, body(): jnp.dot(flat, both.reshape(2 * rows, -1).T, precision=lax.Precision.HIGHEST)  7.79 us
    dot_general x1, matrix products, body(): jnp.dot(inverse, flat, precision=lax.Precision.HIGHEST)  3.8 us

profile of v4, /device:TPU:0, one launch (start us, length us, event | category | flops | bytes accessed | tf_op | source)
XLA Modules:
  0.0 125.6 jit_solution(1671887701863336325)
XLA Ops:
  0.6 0.0 copy-start
  0.6 1.6 %copy-done = f32[64,8,8,128]{3,2,1,0:T(8,128)S(1)} copy-done((f32[64,8,8,128]{3,2,1,0:T(8,128)S(1)}, f32[64,8,8,128]{3,2,1,0:T(8,128)}, u32[]{:S(2)}) %copy-start) | copy-done | bytes 2097176
  2.2 0.0 copy-start.1
  2.2 0.8 copy-done.1
  3.0 0.0 copy-start.2
  3.0 0.7 copy-done.2
  3.7 0.0 copy-start.3
  3.7 0.7 copy-done.3
  4.3 0.0 copy-start.4
  4.3 0.7 copy-done.4
  5.0 85.3 %shard_map.68 = (f32[64,8,8,128]{3,2,1,0:T(8,128)S(1)}, f32[128,8,8,128]{3,2,1,0:T(8,128)S(1)}) custom-call(f32[4]{0:T(128)S(1)} %copy-done.3, f32[4]{0:T(128)S(1)} %copy-done.4, f32[64,8,8,128]{3,2,1,0:T(8,128)S(1)} %copy-done, s32[8,8,128]{2,1,0:T(8,128)S(1)} %copy-done.1, s32[8,128]{1,0:T(8,128)S(1)} %copy-done.2), custom_call_target="tpu_custom_call" | custom-call | tf_op jit(solution)/shard_map/pallas_call | solution.py:207
  90.3 7.8 %fusion.5.local_ref = f32[64,128]{1,0:T(8,128)} fusion(f32[128,8,8,128]{3,2,1,0:T(8,128)S(1)} %get-tuple-element.7, f32[64,8,8,128]{3,2,1,0:T(8,128)S(1)} %get-tuple-element.6), kind=kOutput, calls=%fused_computation.6 | convolution fusion | flops 805306368 | bytes 6324224 | tf_op jit(solution)/shard_map/dot_general | solution.py:348
  98.1 1.2 copy.29
  99.3 0.4 copy.17
  99.7 19.0 %shard_map.69 = (f32[64,64]{1,0:T(8,128)}, f32[64,64]{1,0:T(8,128)}) custom-call(f32[64,128]{1,0:T(8,128)} %fusion.5.local_ref), custom_call_target="tpu_custom_call" | custom-call | tf_op jit(solution)/shard_map/pallas_call | solution.py:287
  118.7 3.8 %fusion.2 = f32[64,8,8,128]{3,0,2,1:T(8,128)S(1)} fusion(f32[8,8,128,64]{2,1,0,3:T(8,128)S(1)} %bitcast.23, f32[64,64]{1,0:T(8,128)} %get-tuple-element.8), kind=kOutput, calls=%fused_computation.3 | convolution fusion | flops 402653184 | bytes 4210688 | tf_op jit(solution)/shard_map/dot_general | solution.py:350
  122.5 0.0 copy-start.5
  122.5 2.5 %copy.13 = f32[64,8,8,128]{3,2,1,0:T(8,128)} copy(f32[64,8,8,128]{3,0,2,1:T(8,128)S(1)} %fusion.2) | data formatting | bytes 4194304
  125.0 0.0 copy-done.5
  125.0 0.6 copy.31
Async XLA Ops:
  0.6 1.6 %copy-start = (f32[64,8,8,128]{3,2,1,0:T(8,128)S(1)}, f32[64,8,8,128]{3,2,1,0:T(8,128)}, u32[]{:S(2)}) copy-start(f32[64,8,8,128]{3,2,1,0:T(8,128)} %init_ref.1) | copy-start | bytes 6291460
  2.2 0.8 copy-start.1
  3.0 0.7 copy-start.2
  3.7 0.7 copy-start.3
  4.3 0.7 copy-start.4
  122.5 2.5 %copy-start.5 = (f32[64,64]{1,0:T(8,128)S(1)}, f32[64,64]{1,0:T(8,128)}, u32[]{:S(2)}) copy-start(f32[64,64]{1,0:T(8,128)} %get-tuple-element.17) | copy-start | bytes 49156
